TPU v7x, 32 devices: a whole 2x2x4 slice. The times are simulated.
32 devices in a mesh: ctx: 16 (over z, x, core), head: 2 (over y).
Axes of the slice: x: 2, y: 2, z: 4, core: 2. Of those that a mesh axis runs over, the one named last changes fastest.
Arguments:
- queries: bfloat16 [4096, 4096], P('ctx', 'head'), may hold values from -180 to 180
- keys: bfloat16 [4096, 1024], P('ctx', 'head'), may hold values from -6.5 to 6.5
- values: bfloat16 [4096, 1024], P('ctx', 'head'), may hold values from -6 to 6
- out_grad: bfloat16 [4096, 4096], P('ctx', 'head'), may hold values from -6 to 6
- attn_out: bfloat16 [4096, 4096], P('ctx', 'head'), may hold values from -6 to 6
- lengths: int32 [16], replicated, may hold values from 1 to 1792, as said below
- proj_weight: bfloat16 [4096, 8, 768], P('ctx', 'head'), may hold values from -0.078125 to 0.078125
Outputs:
- input_grad: bfloat16 [4096, 4096], P('ctx', 'head')
Inputs may be any that keep to these rules, and one draw needn't show every extreme that they name: `lengths`: every document has 1 to 1792 tokens, one has exactly 1792, and they sum to 4096.
All inputs are finite; a program needn't handle non-finite values.
Results may differ from a plain program's by a relative error of at most 0.013.
Values may be sent and summed in bfloat16 or wider, within the bound.
A program may use at most 192 MiB of HBM per device.

v0:
```python
import jax
import jax.numpy as jnp
from jax import lax
from jax.sharding import PartitionSpec as P

HQ = 32
KVH = 8
HD = 128
REACH = 7


def from_behind(array, axis, by):
    peers = lax.axis_size(axis)
    pairs = [(i, i + by) for i in range(peers) if 0 <= i + by < peers]
    return lax.ppermute(array, axis, pairs)


def doc_number(positions, ends):
    counted = jnp.sum((positions[:, None] >= ends[None, :]).astype(jnp.int32), axis=1)
    return jnp.where(positions >= 0, counted, -1)


def shards(queries, keys, values, out_grad, attn_out, lengths, proj_weight):
    tile_len = queries.shape[0]
    heads_here = keys.shape[1] // HD
    group = HQ // KVH
    window = REACH + 1
    scale_factor = HD ** (-0.5)
    position = lax.axis_index("ctx")
    ends = jnp.cumsum(lengths)
    query_pos = position * tile_len + jnp.arange(tile_len, dtype=jnp.int32)
    key_pos = (
        position * tile_len - REACH * tile_len + jnp.arange(window * tile_len, dtype=jnp.int32)
    )
    allowed = (doc_number(query_pos, ends)[:, None] == doc_number(key_pos, ends)[None, :]) & (
        key_pos[None, :] <= query_pos[:, None]
    )
    key_value = jnp.stack([keys, values])
    stacked = key_value
    spread = 1
    while spread < window:
        stacked = jnp.concatenate([from_behind(stacked, "ctx", spread), stacked], axis=1)
        spread = spread * 2
    key_window = stacked[0].reshape(window * tile_len, heads_here, HD)
    value_window = stacked[1].reshape(window * tile_len, heads_here, HD)
    query_tile = queries.reshape(tile_len, heads_here, group, HD)
    dout_tile = out_grad.reshape(tile_len, heads_here, group, HD)
    delta = jnp.sum(
        (out_grad.astype(jnp.float32) * attn_out.astype(jnp.float32)).reshape(
            tile_len, heads_here, group, HD
        ),
        axis=3,
    )
    scores = (
        jnp.einsum("tkgd,ukd->kgtu", query_tile, key_window, preferred_element_type=jnp.float32)
        * scale_factor
    )
    row_max = jnp.max(jnp.where(allowed[None, None], scores, -1e30), axis=3, keepdims=True)
    total = jnp.sum(
        jnp.where(allowed[None, None], jnp.exp(scores - row_max), 0.0), axis=3, keepdims=True
    )
    lse_tile = row_max + jnp.log(total)
    probs = jnp.where(allowed[None, None], jnp.exp(scores - lse_tile), 0.0)
    probs_low = probs.astype(jnp.bfloat16)
    value_grad = jnp.einsum(
        "kgtu,tkgd->ukd", probs_low, dout_tile, preferred_element_type=jnp.float32
    )
    dprobs = jnp.einsum(
        "tkgd,ukd->kgtu", dout_tile, value_window, preferred_element_type=jnp.float32
    )
    delta_here = jnp.transpose(delta, (1, 2, 0))[..., None]
    dscore = (probs * (dprobs - delta_here) * scale_factor).astype(jnp.bfloat16)
    query_grad = jnp.einsum(
        "kgtu,ukd->tkgd", dscore, key_window, preferred_element_type=jnp.float32
    ).astype(jnp.bfloat16)
    key_grad = jnp.einsum("kgtu,tkgd->ukd", dscore, query_tile, preferred_element_type=jnp.float32)
    grad_window = jnp.stack([key_grad, value_grad]).reshape(2, window * tile_len, heads_here * HD)
    owned = grad_window
    spread = window
    while spread > 1:
        half_len = spread // 2
        owned = owned[:, half_len * tile_len :] + from_behind(
            owned[:, : half_len * tile_len], "ctx", -half_len
        )
        spread = half_len
    key_final = owned[0].astype(jnp.bfloat16).reshape(tile_len, heads_here, HD)
    value_final = owned[1].astype(jnp.bfloat16).reshape(tile_len, heads_here, HD)
    combined = jnp.concatenate(
        [query_grad.reshape(tile_len, heads_here, group * HD), key_final, value_final], axis=2
    ).reshape(tile_len, -1)
    weights = proj_weight.reshape(proj_weight.shape[0], -1)
    partial_sum = lax.dot_general(
        combined,
        lax.all_gather(weights, "ctx", axis=0, tiled=True),
        (((1,), (1,)), ((), ())),
        preferred_element_type=jnp.float32,
    )
    summed = lax.psum_scatter(
        partial_sum.astype(jnp.bfloat16), "head", scatter_dimension=1, tiled=True
    )
    return summed


def solution(mesh):
    placed = (
        P("ctx", "head"),
        P("ctx", "head"),
        P("ctx", "head"),
        P("ctx", "head"),
        P("ctx", "head"),
        P(),
        P("ctx", "head", None),
    )
    return jax.shard_map(
        shards, mesh=mesh, in_specs=placed, out_specs=P("ctx", "head"), check_vma=False
    )
```

profile of v0, /device:TPU:0, one launch (start us, length us, event | category | flops | bytes accessed | tf_op | source)
XLA Modules:
  0.0 465.7 jit_solution(11620687411967607157)
XLA Ops:
  6.5 0.0 all-gather.2.cloned.1.call-start
  6.5 2.9 copy.69
  9.4 0.0 all-gather.2.cloned.1.call-update
  9.5 0.0 copy-start.7
  9.5 0.0 reduce-scatter.2.cloned.1.call-start
  9.5 0.0 copy-done.10
  9.5 0.1 copy.43
  9.7 0.0 copy-done.11
  9.7 0.1 copy.42
  9.8 0.1 pad_maximum_fusion.2
  9.9 0.0 copy-start.12
  9.9 2.5 collective-permute-start
  12.4 1.5 collective-permute-done
  13.9 0.1 maximum_maximum_fusion.2
  14.0 16.0 %collective-permute-start.1 = (bf16[2,512,512]{1,2,0:T(8,128)(2,1)S(1)}, bf16[2,512,512]{1,2,0:T(8,128)(2,1)S(1)}, u32[]{:S(2)}, u32[]{:S(2)}) collective-permute-start(bf16[2,512,512]{1,2,0:T(8,128)(2,1)S(1)} %maximum_maximum_fusion.2), channel_id=1, source_target_pairs={{0,4},{2,6},{4,8},{6,10},{8,12},{10,14},{12,16},{14,18},{16,20},{1... | collective-permute-start | bytes 3145736 | tf_op jit(solution)/shard_map/ppermute | solution.py:15
  30.0 45.2 %collective-permute-done.1 = bf16[2,512,512]{1,2,0:T(8,128)(2,1)S(1)} collective-permute-done((bf16[2,512,512]{1,2,0:T(8,128)(2,1)S(1)}, bf16[2,512,512]{1,2,0:T(8,128)(2,1)S(1)}, u32[]{:S(2)}, u32[]{:S(2)}) %collective-permute-start.1) | collective-permute-done | bytes 1048608 | tf_op jit(solution)/shard_map/ppermute | solution.py:15
  75.2 1.7 maximum_maximum_fusion.1
  76.9 6.7 %collective-permute-start.2 = (bf16[2,1024,512]{1,2,0:T(8,128)(2,1)}, bf16[2,1024,512]{1,2,0:T(8,128)(2,1)}, u32[]{:S(2)}, u32[]{:S(2)}) collective-permute-start(bf16[2,1024,512]{1,2,0:T(8,128)(2,1)} %maximum_maximum_fusion.1), channel_id=1, source_target_pairs={{0,8},{2,10},{4,12},{6,14},{8,16},{10,18},{12,20},{14,22},{16,24},... | collective-permute-start | bytes 6291464 | tf_op jit(solution)/shard_map/ppermute | solution.py:15
  83.6 1.3 copy.68
  84.9 0.0 copy-done.5
  84.9 0.1 copy.44
  85.0 0.1 reduce
  85.1 1.5 copy.67
  86.6 3.3 convert_multiply_fusion
  89.9 2.8 reshape.146
  92.8 2.4 reduce_sum.39
  95.1 1.2 copy.49
  96.4 0.1 convert_reduce_fusion.1
  96.5 0.1 convert_reduce_fusion
  96.6 1.4 compare_and_fusion
  98.0 72.9 %collective-permute-done.2 = bf16[2,1024,512]{1,2,0:T(8,128)(2,1)} collective-permute-done((bf16[2,1024,512]{1,2,0:T(8,128)(2,1)}, bf16[2,1024,512]{1,2,0:T(8,128)(2,1)}, u32[]{:S(2)}, u32[]{:S(2)}) %collective-permute-start.2) | collective-permute-done | bytes 2097184 | tf_op jit(solution)/shard_map/ppermute | solution.py:15
  171.0 2.4 maximum_maximum_fusion
  173.4 1.9 fusion.18
  175.3 13.7 %fusion.3 = (f32[4,4,256]{2,1,0:T(4,128)S(1)}, f32[4,2048,256,4]{2,1,3,0:T(8,128)}) fusion(pred[256,2048]{0,1:T(8,128)(4,1)S(1)} %compare_and_fusion, bf16[2048,4,128,1]{0,2,3,1:T(8,128)(2,1)S(1)} %bitcast.86, bf16[256,4,4,128]{0,3,2,1:T(8,128)(2,1)S(1)} %bitcast.90), kind=kOutput, calls=%fused_computation.7 | convolution fusion | flops 2172645376 | bytes 37240832 | tf_op jit(solution)/shard_map/tkgd,ukd->kgtu/dot_general | solution.py:55
  189.0 14.4 %fusion.6 = f32[4,4,256]{2,1,0:T(4,128)S(1)} fusion(f32[4,2048,256,4]{2,1,3,0:T(8,128)} %get-tuple-element.10, f32[4,4,256]{2,1,0:T(4,128)S(1)} %get-tuple-element.9, pred[256,2048]{0,1:T(8,128)(4,1)S(1)} %compare_and_fusion), kind=kLoop, calls=%fused_computation.10 | loop fusion | flops 33550336 | bytes 34111488 | tf_op jit(solution)/shard_map/reduce_sum | solution.py:59
  203.4 17.3 %fusion.2 = bf16[4,4,256,2048]{2,3,1,0:T(8,128)(2,1)S(1)} fusion(f32[4,2048,256,4]{2,1,3,0:T(8,128)} %get-tuple-element.10, bf16[2048,4,128,1]{0,2,3,1:T(8,128)(2,1)} %bitcast.103, bf16[256,4,4,128]{0,3,2,1:T(8,128)(2,1)S(1)} %bitcast.107, f32[4,4,256]{2,1,0:T(4,128)S(1)} %copy.49, f32[4,4,256]{2,1,0:T(4,128)S(1)} %bitcast.112, ...), kind=kOutput, calls=%fused_computation.3 | convolution fusion | flops 2206203904 | bytes 54034432 | tf_op jit(solution)/shard_map/tkgd,ukd->kgtu/dot_general | solution.py:68
  220.7 5.7 %copy-done = bf16[4,4,256,2048]{2,3,1,0:T(8,128)(2,1)} copy-done((bf16[4,4,256,2048]{2,3,1,0:T(8,128)(2,1)}, bf16[4,4,256,2048]{2,3,1,0:T(8,128)(2,1)S(1)}, u32[]{:S(2)}) %copy-start) | copy-done | bytes 16777240
  226.4 8.8 %fusion.20 = f32[4,2048,128,1]{1,2,3,0:T(8,128)} fusion(bf16[4,4,256,2048]{2,3,1,0:T(8,128)(2,1)S(1)} %fusion.2, bf16[256,4,4,128]{0,3,2,1:T(8,128)(2,1)} %bitcast.91), kind=kOutput, calls=%fused_computation.44 | convolution fusion | flops 2147483648 | bytes 22020096 | tf_op jit(solution)/shard_map/kgtu,tkgd->ukd/dot_general | solution.py:76
  235.2 16.5 %fusion.10 = f32[4,2048,128,1]{1,2,3,0:T(8,128)} fusion(bf16[256,4,4,128]{0,3,2,1:T(8,128)(2,1)} %bitcast.106, f32[4,2048,256,4]{2,1,3,0:T(8,128)} %get-tuple-element.10, f32[4,4,256]{2,1,0:T(4,128)S(1)} %bitcast.113, pred[256,2048]{0,1:T(8,128)(4,1)S(1)} %compare_and_fusion), kind=kOutput, calls=%fused_computation.14 | convolution fusion | flops 2181038080 | bytes 39337984 | tf_op jit(solution)/shard_map/kgtu,tkgd->ukd/dot_general | solution.py:65
  251.7 2.7 pad_maximum_fusion
  254.4 0.0 slice-start.2
  254.4 1.6 collective-permute-start.3
  256.0 89.5 %collective-permute-done.3 = f32[2,1024,512]{1,2,0:T(8,128)S(1)} collective-permute-done((f32[2,1024,512]{1,2,0:T(8,128)S(1)}, f32[2,1024,512]{1,2,0:T(8,128)S(1)}, u32[]{:S(2)}, u32[]{:S(2)}) %collective-permute-start.3) | collective-permute-done | bytes 4194336 | tf_op jit(solution)/shard_map/ppermute | solution.py:15
  345.5 2.7 fusion.14
  348.2 0.0 slice-start.3
  348.2 0.2 slice.47
  348.5 1.6 collective-permute-start.4
  350.0 45.3 %collective-permute-done.4 = f32[2,512,512]{1,2,0:T(8,128)S(1)} collective-permute-done((f32[2,512,512]{1,2,0:T(8,128)S(1)}, f32[2,512,512]{1,2,0:T(8,128)S(1)}, u32[]{:S(2)}, u32[]{:S(2)}) %collective-permute-start.4) | collective-permute-done | bytes 2097184 | tf_op jit(solution)/shard_map/ppermute | solution.py:15
  395.3 0.5 slice_add_fusion
  395.8 0.1 slice.49
  395.9 1.3 collective-permute-start.5
  397.2 0.0 slice-done
  397.2 0.0 slice-done.1
  397.2 0.0 slice-done.2
  397.2 0.0 slice-done.3
  397.3 0.0 copy-done.3
  397.3 2.4 convolution_convert_fusion.1
  399.6 0.8 collective-permute-done.5
  400.5 0.2 fusion.15
  400.7 0.1 pad_maximum_fusion.1
  400.8 0.0 all-gather.2.cloned.1.call-done
  400.9 13.5 %convolution_convert_fusion = bf16[256,4096]{1,0:T(8,128)(2,1)} fusion(bf16[256,3072]{0,1:T(8,128)(2,1)S(1)} %bitcast.105, bf16[4096,3072]{1,0:T(8,128)(2,1)} %all-gather.2.cloned.1.call-done), kind=kOutput, calls=%fused_computation.18 | convolution fusion | flops 6443499520 | bytes 28835840 | tf_op jit(solution)/shard_map/dot_general | solution.py:92
  414.3 0.0 reduce-scatter.2.cloned.1.call-update
  414.4 44.5 %reduce-scatter.2.cloned.1.call-done = bf16[256,2048]{1,0:T(8,128)(2,1)} async-done(((bf16[256,4096]{1,0:T(8,128)(2,1)}), bf16[256,2048]{1,0:T(8,128)(2,1)}) %reduce-scatter.2.cloned.1.call-update) | async-done | bytes 1048592 | tf_op jit(solution)/shard_map/reduce_scatter | solution.py:98
  (29 shorter events, 0.1 us)
Async XLA Ops:
  6.5 3.0 copy-start.10
  6.5 3.1 copy-start.11
  6.5 394.3 %all-gather.2.cloned.1.call-start = ((), (), s32[]{:S(2)}) async-start(), calls=%async_computation.1 | async-start | bytes 26738688 | tf_op jit(solution)/shard_map/all_gather | solution.py:94
  9.5 74.1 %copy-start.7 = (bf16[256,2048]{1,0:T(8,128)(2,1)S(1)}, bf16[256,2048]{1,0:T(8,128)(2,1)}, u32[]{:S(2)}) copy-start(bf16[256,2048]{1,0:T(8,128)(2,1)} %param.10) | copy-start | bytes 3145732
  9.5 449.3 %reduce-scatter.2.cloned.1.call-start = ((), (), s32[]{:S(2)}) async-start(), calls=%async_computation.2 | async-start | bytes 3145728 | tf_op jit(solution)/shard_map/reduce_scatter | solution.py:98
  9.8 75.1 %copy-start.5 = (bf16[256,512]{0,1:T(8,128)(2,1)}, bf16[256,512]{0,1:T(8,128)(2,1)S(1)}, u32[]{:S(2)}) copy-start(bf16[256,512]{0,1:T(8,128)(2,1)S(1)} %copy.42) | copy-start | bytes 786436
  9.9 75.0 %copy-start.12 = (s32[16]{0:T(128)S(1)}, s32[16]{0:T(128)}, u32[]{:S(2)}) copy-start(s32[16]{0:T(128)} %param.12) | copy-start | bytes 196
  9.9 4.0 collective-permute-start
  13.9 71.0 %copy-start.6 = (bf16[2,256,512]{1,2,0:T(8,128)(2,1)}, bf16[2,256,512]{1,2,0:T(8,128)(2,1)S(1)}, u32[]{:S(2)}) copy-start(bf16[2,256,512]{1,2,0:T(8,128)(2,1)S(1)} %collective-permute-done) | copy-start | bytes 1572868
  14.0 61.2 %collective-permute-start.1 = (bf16[2,512,512]{1,2,0:T(8,128)(2,1)S(1)}, bf16[2,512,512]{1,2,0:T(8,128)(2,1)S(1)}, u32[]{:S(2)}, u32[]{:S(2)}) collective-permute-start(bf16[2,512,512]{1,2,0:T(8,128)(2,1)S(1)} %maximum_maximum_fusion.2), channel_id=1, source_target_pairs={{0,4},{2,6},{4,8},{6,10},{8,12},{10,14},{12,16},{14,18},{16,20},{1... | collective-permute-start | bytes 3145736 | tf_op jit(solution)/shard_map/ppermute | solution.py:15
  75.2 11.4 %copy-start.8 = (bf16[2,512,512]{1,2,0:T(8,128)(2,1)}, bf16[2,512,512]{1,2,0:T(8,128)(2,1)S(1)}, u32[]{:S(2)}) copy-start(bf16[2,512,512]{1,2,0:T(8,128)(2,1)S(1)} %collective-permute-done.1) | copy-start | bytes 3145732
  76.9 94.1 %collective-permute-start.2 = (bf16[2,1024,512]{1,2,0:T(8,128)(2,1)}, bf16[2,1024,512]{1,2,0:T(8,128)(2,1)}, u32[]{:S(2)}, u32[]{:S(2)}) collective-permute-start(bf16[2,1024,512]{1,2,0:T(8,128)(2,1)} %maximum_maximum_fusion.1), channel_id=1, source_target_pairs={{0,8},{2,10},{4,12},{6,14},{8,16},{10,18},{12,20},{14,22},{16,24},... | collective-permute-start | bytes 6291464 | tf_op jit(solution)/shard_map/ppermute | solution.py:15
  86.6 88.7 %copy-start.4 = (bf16[256,2048]{0,1:T(8,128)(2,1)}, bf16[256,2048]{0,1:T(8,128)(2,1)S(1)}, u32[]{:S(2)}) copy-start(bf16[256,2048]{0,1:T(8,128)(2,1)S(1)} %copy.67) | copy-start | bytes 3145732
  175.3 13.7 %copy-start.2 = (bf16[1,2048,512]{1,2,0:T(8,128)(2,1)}, bf16[1,2048,512]{1,2,0:T(8,128)(2,1)S(1)}, u32[]{:S(2)}) copy-start(bf16[1,2048,512]{1,2,0:T(8,128)(2,1)S(1)} %get-tuple-element.6) | copy-start | bytes 6291460
  189.0 14.4 %copy-start.9 = (bf16[256,2048]{0,1:T(8,128)(2,1)S(1)}, bf16[256,2048]{0,1:T(8,128)(2,1)}, u32[]{:S(2)}) copy-start(bf16[256,2048]{0,1:T(8,128)(2,1)} %copy.68) | copy-start | bytes 3145732
  220.7 5.7 %copy-start = (bf16[4,4,256,2048]{2,3,1,0:T(8,128)(2,1)}, bf16[4,4,256,2048]{2,3,1,0:T(8,128)(2,1)S(1)}, u32[]{:S(2)}) copy-start(bf16[4,4,256,2048]{2,3,1,0:T(8,128)(2,1)S(1)} %fusion.2) | copy-start | bytes 50331652
  251.7 93.8 %copy-start.1 = (f32[4,2048,128,1]{1,2,3,0:T(8,128)S(1)}, f32[4,2048,128,1]{1,2,3,0:T(8,128)}, u32[]{:S(2)}) copy-start(f32[4,2048,128,1]{1,2,3,0:T(8,128)} %fusion.20) | copy-start | bytes 12582916
  251.7 145.5 %slice-start = ((s8[16777216]{0:T(1024)(128)(4,1)}), s8[4194304]{0:T(1024)(128)(4,1)S(1)}, s32[]{:S(2)}) async-start(s8[16777216]{0:T(1024)(128)(4,1)} %bitcast.82), calls=%async_computation.3 | async-start | bytes 8388608
  251.7 145.5 %slice-start.1 = ((s8[16777216]{0:T(1024)(128)(4,1)}), s8[4194304]{0:T(1024)(128)(4,1)S(1)}, s32[]{:S(2)}) async-start(s8[16777216]{0:T(1024)(128)(4,1)} %bitcast.82), calls=%async_computation.4 | async-start | bytes 8388608
  254.4 142.8 %slice-start.2 = ((s8[16777216]{0:T(1024)(128)(4,1)}), s8[4194304]{0:T(1024)(128)(4,1)S(1)}, s32[]{:S(2)}) async-start(s8[16777216]{0:T(1024)(128)(4,1)} %bitcast.82), calls=%async_computation.5 | async-start | bytes 8388608
  254.4 91.1 %collective-permute-start.3 = (f32[2,1024,512]{1,2,0:T(8,128)S(1)}, f32[2,1024,512]{1,2,0:T(8,128)S(1)}, u32[]{:S(2)}, u32[]{:S(2)}) collective-permute-start(f32[2,1024,512]{1,2,0:T(8,128)S(1)} %pad_maximum_fusion), channel_id=1, source_target_pairs={{8,0},{10,2},{12,4},{14,6},{16,8},{18,10},{20,12},{22,14},{24,16},... | collective-permute-start | bytes 12582920 | tf_op jit(solution)/shard_map/ppermute | solution.py:15
  348.2 49.0 %slice-start.3 = ((s8[16777216]{0:T(1024)(128)(4,1)}), s8[4194304]{0:T(1024)(128)(4,1)S(1)}, s32[]{:S(2)}) async-start(s8[16777216]{0:T(1024)(128)(4,1)} %bitcast.82), calls=%async_computation.6 | async-start | bytes 8388608
  348.5 48.8 %copy-start.3 = (bf16[1,2048,512]{1,2,0:T(8,128)(2,1)S(1)}, bf16[1,2048,512]{1,2,0:T(8,128)(2,1)}, u32[]{:S(2)}) copy-start(bf16[1,2048,512]{1,2,0:T(8,128)(2,1)} %copy-done.2) | copy-start | bytes 6291460
  348.5 46.9 %collective-permute-start.4 = (f32[2,512,512]{1,2,0:T(8,128)S(1)}, f32[2,512,512]{1,2,0:T(8,128)S(1)}, u32[]{:S(2)}, u32[]{:S(2)}) collective-permute-start(f32[2,512,512]{1,2,0:T(8,128)S(1)} %slice.47), channel_id=1, source_target_pairs={{4,0},{6,2},{8,4},{10,6},{12,8},{14,10},{16,12},{18,14},{20,16},{2... | collective-permute-start | bytes 6291464 | tf_op jit(solution)/shard_map/ppermute | solution.py:15
  395.9 4.6 collective-permute-start.5
Sparse Core Ops, SparseCore 0:
  9.6 179.6 all-gather.1
  414.5 44.2 reduce-scatter.1
where the time goes:
time: 466 us
  waiting for transfers between devices  300 us (64%)
  matrix products  72.1 us (15%)
  other arithmetic  32.3 us (7%)
  starting transfers between devices  29.7 us (6%)
  local copies, waits for them, and re-layouts  18.1 us (4%)
  between operations  13.8 us (3%)
    ppermute x6, waiting for transfers between devices, from_behind(): return lax.ppermute(array, axis, pairs)  255 us
    reduce_scatter x1, waiting for transfers between devices, shards(): lax.psum_scatter(partial_sum.astype(jnp.bfloat16), 'head', scatter_dimens...  44.5 us
    ppermute x6, starting transfers between devices, from_behind(): return lax.ppermute(array, axis, pairs)  29.6 us
    dot_general x1, matrix products, shards(): jnp.einsum('tkgd,ukd->kgtu', dout_tile, value_window, preferred_element_t...  17.3 us
    dot_general x1, matrix products, shards(): jnp.einsum('kgtu,tkgd->ukd', probs_low, dout_tile, preferred_element_type...  16.5 us
    reduce_sum x1, other arithmetic, shards(): jnp.sum(jnp.where(allowed[None, None], jnp.exp(scores - row_max), 0.0), a...  14.4 us
    dot_general x1, matrix products, shards(): jnp.einsum('tkgd,ukd->kgtu', query_tile, key_window, preferred_element_ty...  13.7 us
    dot_general x1, matrix products, shards(): lax.dot_general(combined, lax.all_gather(weights, 'ctx', axis=0, tiled=Tr...  13.5 us
  transfers between devices with their start and end apart: 8, of which 7 were waited for; matrix products, arithmetic and copies ran while one was open for 22% of the time, Pallas kernels for 0%

commit v1 on v0

v1 whole, which is shorter than its diff:
```python
import functools
import math

import jax
import jax.numpy as jnp
from jax import lax
from jax.experimental import pallas as pl
from jax.experimental.pallas import tpu as pltpu
from jax.sharding import PartitionSpec as P

HQ = 32
KVH = 8
HD = 128
GROUP = HQ // KVH
QUAD = 4
REACH = 7
NSLOT = 3 * QUAD
MESH = pl.DeviceIdType.MESH
NEG = -1e30


def place(n):
    c = lax.axis_index("ctx")
    m = c // QUAD
    b = (c // 2) % 2
    k = c % 2
    return c, m, b, k, n // QUAD


def greet(n):
    c, m, b, k, quads = place(n)
    barrier = pltpu.get_barrier_semaphore()

    def hello(peer):
        pl.semaphore_signal(barrier, inc=1, device_id={"ctx": peer}, device_id_type=MESH)

    hello(c + 2 - 4 * b)
    hello(c + 1 - 2 * k)

    @pl.when(m > 0)
    def _():
        hello(c - QUAD)

    @pl.when(m < quads - 1)
    def _():
        hello(c + QUAD)

    pl.semaphore_wait(barrier, 2 + jnp.where(m > 0, 1, 0) + jnp.where(m < quads - 1, 1, 0))


def remote(src, dst, send, recv, peer):
    return pltpu.make_async_remote_copy(
        src_ref=src, dst_ref=dst, send_sem=send, recv_sem=recv,
        device_id={"ctx": peer}, device_id_type=MESH)


def gather_kernel(n, kv_ref, out_ref, own_sem, send, recv):
    c, m, b, k, quads = place(n)
    up, other, sib = c + QUAD, c + 2 - 4 * b, c + 1 - 2 * k
    greet(n)

    def slot(dz, bb, kk):
        return out_ref.at[(2 - dz) * QUAD + 2 * bb + kk]

    def has(dz):
        return m >= dz

    def x_from(dz):
        return (b == 0, b >= 0, b == 1)[dz]

    def x_to(dz):
        return (b == 1, b >= 0, b == 0)[dz]

    def z_copy(dz):
        src = kv_ref if dz == 0 else slot(dz, b, k)
        return remote(src, slot(dz + 1, b, k), send.at[dz, 0], recv.at[dz + 1, 0], up)

    def s_copy(dz):
        src = kv_ref if dz == 0 else slot(dz, b, k)
        return remote(src, slot(dz, b, k), send.at[dz, 1], recv.at[dz, 1], sib)

    def x_copy(dz):
        src = kv_ref if dz == 0 else slot(dz, b, k)
        return remote(src, slot(dz, b, k), send.at[dz, 2], recv.at[dz, 2], other)

    def f_copy(dz):
        return remote(slot(dz, 1 - b, k), slot(dz, 1 - b, k), send.at[dz, 3], recv.at[dz, 3], sib)

    own = pltpu.make_async_copy(kv_ref, slot(0, b, k), own_sem)
    own.start()
    for dz in range(3):
        @pl.when(has(dz))
        def _(dz=dz):
            if dz > 0:
                z_copy(dz - 1).wait_recv()
            if dz < 2:
                @pl.when(m < quads - 1)
                def _():
                    z_copy(dz).start()

            @pl.when(x_from(dz))
            def _():
                x_copy(dz).start()
            s_copy(dz).start()

        if dz > 0:
            @pl.when(jnp.logical_and(has(dz - 1), x_to(dz - 1)))
            def _(dz=dz):
                x_copy(dz - 1).wait_recv()
                f_copy(dz - 1).start()

    @pl.when(jnp.logical_and(has(2), x_to(2)))
    def _():
        x_copy(2).wait_recv()
        f_copy(2).start()

    for dz in range(3):
        @pl.when(has(dz))
        def _(dz=dz):
            s_copy(dz).wait_recv()
            s_copy(dz).wait_send()
            if dz < 2:
                @pl.when(m < quads - 1)
                def _():
                    z_copy(dz).wait_send()

            @pl.when(x_from(dz))
            def _():
                x_copy(dz).wait_send()

            @pl.when(x_to(dz))
            def _():
                f_copy(dz).wait_recv()
                f_copy(dz).wait_send()
    own.wait()


def gather_window(n, kv):
    return pl.pallas_call(
        functools.partial(gather_kernel, n),
        out_shape=jax.ShapeDtypeStruct((NSLOT,) + kv.shape, kv.dtype),
        in_specs=[pl.BlockSpec(memory_space=pltpu.VMEM)],
        out_specs=pl.BlockSpec(memory_space=pltpu.VMEM),
        scratch_shapes=[
            pltpu.SemaphoreType.DMA,
            pltpu.SemaphoreType.DMA((3, 4)),
            pltpu.SemaphoreType.DMA((3, 4)),
        ],
        compiler_params=pltpu.CompilerParams(
            collective_id=0, has_side_effects=True, vmem_limit_bytes=32 * 1024 * 1024),
    )(kv)


def reduce_kernel(n, g_ref, out_ref, from_f, from_s, from_x, from_z, sum_x, sum_z, send, recv):
    c, m, b, k, quads = place(n)
    down, other, sib = c - QUAD, c + 2 - 4 * b, c + 1 - 2 * k
    greet(n)

    def part(dz, bb, kk):
        return g_ref.at[(2 - dz) * QUAD + 2 * bb + kk]

    def has(dz):
        return m >= dz

    def x_to(dz):
        return (b == 0, b >= 0, b == 1)[dz]

    def x_from(dz):
        return (b == 1, b >= 0, b == 0)[dz]

    def f_copy(dz):
        return remote(part(dz, 1 - b, 1 - k), from_f.at[dz], send.at[dz, 3], recv.at[dz, 3], sib)

    def s_copy(dz):
        return remote(part(dz, b, 1 - k), from_s.at[dz], send.at[dz, 1], recv.at[dz, 1], sib)

    def x_copy(dz):
        return remote(sum_x.at[dz], from_x.at[dz], send.at[dz, 2], recv.at[dz, 2], other)

    def z_copy(dz):
        return remote(sum_z.at[dz], from_z.at[dz - 1], send.at[dz, 0], recv.at[dz - 1, 0], down)

    for dz in (2, 1, 0):
        @pl.when(has(dz))
        def _(dz=dz):
            @pl.when(x_from(dz))
            def _():
                f_copy(dz).start()
            s_copy(dz).start()

    for dz in (2, 1, 0):
        @pl.when(jnp.logical_and(has(dz), x_from(dz)))
        def _(dz=dz):
            f_copy(dz).wait_recv()
            sum_x[dz] = (part(dz, 1 - b, k)[...].astype(jnp.float32)
                         + from_f[dz].astype(jnp.float32)).astype(sum_x.dtype)
            x_copy(dz).start()

    for dz in (2, 1, 0):
        @pl.when(has(dz))
        def _(dz=dz):
            s_copy(dz).wait_recv()
            sum_z[dz] = (part(dz, b, k)[...].astype(jnp.float32)
                         + from_s[dz].astype(jnp.float32)).astype(sum_z.dtype)

            @pl.when(x_to(dz))
            def _():
                x_copy(dz).wait_recv()
                sum_z[dz] = (sum_z[dz].astype(jnp.float32)
                             + from_x[dz].astype(jnp.float32)).astype(sum_z.dtype)
            if dz < 2:
                @pl.when(m < quads - 1)
                def _():
                    z_copy(dz + 1).wait_recv()
                    sum_z[dz] = (sum_z[dz].astype(jnp.float32)
                                 + from_z[dz].astype(jnp.float32)).astype(sum_z.dtype)
            if dz > 0:
                z_copy(dz).start()

    out_ref[...] = sum_z[0]
    for dz in range(3):
        @pl.when(has(dz))
        def _(dz=dz):
            s_copy(dz).wait_send()

            @pl.when(x_from(dz))
            def _():
                f_copy(dz).wait_send()
                x_copy(dz).wait_send()
            if dz > 0:
                z_copy(dz).wait_send()


def reduce_window(n, parts):
    one = parts.shape[1:]
    vmem = pl.BlockSpec(memory_space=pltpu.VMEM)
    return pl.pallas_call(
        functools.partial(reduce_kernel, n),
        out_shape=jax.ShapeDtypeStruct(one, parts.dtype),
        in_specs=[vmem],
        out_specs=vmem,
        scratch_shapes=[pltpu.VMEM((count,) + one, parts.dtype) for count in (3, 3, 3, 2, 3, 3)] + [
            pltpu.SemaphoreType.DMA((3, 4)),
            pltpu.SemaphoreType.DMA((3, 4)),
        ],
        compiler_params=pltpu.CompilerParams(
            collective_id=1, has_side_effects=True, vmem_limit_bytes=40 * 1024 * 1024),
    )(parts)


def dot(a, b, ca, cb, **kw):
    return lax.dot_general(a, b, (((ca,), (cb,)), ((), ())), preferred_element_type=jnp.float32, **kw)


def attention_kernel(info, q_ref, do_ref, ao_ref, kv_ref, rows_ref, dq_ref, g_ref,
                     qs, dos, s_ref, dqt):
    tile = q_ref.shape[0]
    wide = GROUP * tile
    scale = HD ** (-0.5)
    rate = scale * math.log2(math.e)
    first, own, base = info[0], info[1], info[2]
    prod = do_ref[...].astype(jnp.float32) * ao_ref[...].astype(jnp.float32)
    ones = jnp.ones((8, HD), jnp.float32)
    deltas = []
    for h in range(GROUP):
        cols = slice(h * HD, (h + 1) * HD)
        qs[h * tile:(h + 1) * tile, :] = q_ref[:, cols]
        dos[h * tile:(h + 1) * tile, :] = do_ref[:, cols]
        deltas.append(dot(ones, prod[:, cols], 1, 1, precision=lax.Precision.HIGHEST)[0:1])
    delta = jnp.concatenate(deltas, axis=1)
    start, stop = rows_ref[0:1, :], rows_ref[1:2, :]
    g_ref[...] = jnp.zeros_like(g_ref)
    dqt[...] = jnp.zeros_like(dqt)

    def block(j):
        return pl.ds(pl.multiple_of(j * tile, tile), tile)

    def scan(j, carry):
        top, total = carry
        s = dot(kv_ref[j, 0], qs[...], 1, 1)
        key = base + j * tile + lax.broadcasted_iota(jnp.int32, s.shape, 0)
        s = jnp.where((key >= start) & (key <= stop), s, NEG)
        s_ref[block(j), :] = s
        new = jnp.maximum(top, jnp.max(s, axis=0, keepdims=True))
        here = jnp.sum(jnp.exp2((s - new) * rate), axis=0, keepdims=True)
        return new, total * jnp.exp2((top - new) * rate) + here

    top, total = scan(own, (jnp.full((1, wide), NEG, jnp.float32), jnp.zeros((1, wide), jnp.float32)))
    top, total = lax.fori_loop(first, own, scan, (top, total))
    inverse = 1.0 / total

    def back(j, carry):
        p = jnp.exp2((s_ref[block(j), :] - top) * rate) * inverse
        dp = dot(kv_ref[j, 1], dos[...], 1, 1)
        ds = (p * (dp - delta)).astype(jnp.bfloat16)
        g_ref[j, 1] = dot(p.astype(jnp.bfloat16), dos[...], 1, 0).astype(g_ref.dtype)
        g_ref[j, 0] = (dot(ds, qs[...], 1, 0) * scale).astype(g_ref.dtype)
        dqt[...] += dot(kv_ref[j, 0], ds, 0, 0)
        return carry

    lax.fori_loop(first, own + 1, back, 0)
    dq = jnp.transpose(dqt[...] * scale)
    for h in range(GROUP):
        dq_ref[:, h * HD:(h + 1) * HD] = dq[h * tile:(h + 1) * tile].astype(dq_ref.dtype)


def attention(info, q, do, ao, window, rows):
    tile = q.shape[0]
    groups = q.shape[1] // (GROUP * HD)
    wide = GROUP * tile
    head = pl.BlockSpec((tile, GROUP * HD), lambda g, info: (0, g))
    slots = pl.BlockSpec((NSLOT, 2, tile, HD), lambda g, info: (0, 0, 0, g))
    return pl.pallas_call(
        attention_kernel,
        grid_spec=pltpu.PrefetchScalarGridSpec(
            num_scalar_prefetch=1,
            grid=(groups,),
            in_specs=[head, head, head, slots, pl.BlockSpec((8, wide), lambda g, info: (0, 0))],
            out_specs=[head, slots],
            scratch_shapes=[
                pltpu.VMEM((wide, HD), jnp.bfloat16),
                pltpu.VMEM((wide, HD), jnp.bfloat16),
                pltpu.VMEM((NSLOT * tile, wide), jnp.float32),
                pltpu.VMEM((HD, wide), jnp.float32),
            ],
        ),
        out_shape=[
            jax.ShapeDtypeStruct(q.shape, q.dtype),
            jax.ShapeDtypeStruct(window.shape, window.dtype),
        ],
        compiler_params=pltpu.CompilerParams(vmem_limit_bytes=48 * 1024 * 1024),
        cost_estimate=pl.CostEstimate(
            flops=10 * NSLOT * tile * wide * HD * groups,
            bytes_accessed=4 * window.size + 8 * q.size, transcendentals=0),
    )(info, q, do, ao, window, rows)


def shards(n, queries, keys, values, out_grad, attn_out, lengths, proj_weight):
    tile = queries.shape[0]
    heads_here = keys.shape[1] // HD
    position = lax.axis_index("ctx")
    weights = lax.all_gather(
        proj_weight.reshape(proj_weight.shape[0], -1), "ctx", axis=0, tiled=True)
    window = gather_window(n, jnp.stack([keys, values]))

    ends = jnp.cumsum(lengths)
    query_pos = position * tile + jnp.arange(tile, dtype=jnp.int32)
    start = jnp.max(jnp.where(ends[None, :] <= query_pos[:, None], ends[None, :], 0), axis=1)
    base = (position // QUAD - 2) * QUAD * tile
    own = 2 * QUAD + position % QUAD
    first = jnp.maximum((start[0] - base) // tile, 0)
    info = jnp.stack([first, own, base]).astype(jnp.int32)
    rows = jnp.stack([start, query_pos] + [query_pos] * 6).astype(jnp.int32)
    rows = jnp.tile(rows, (1, GROUP))
    dq, parts = attention(info, queries, out_grad, attn_out, window, rows)
    grads = reduce_window(n, parts)
    combined = jnp.concatenate(
        [dq.reshape(tile, heads_here, GROUP * HD),
         grads[0].reshape(tile, heads_here, HD),
         grads[1].reshape(tile, heads_here, HD)], axis=2).reshape(tile, -1)
    partial_sum = lax.dot_general(
        combined, weights, (((1,), (1,)), ((), ())), preferred_element_type=jnp.float32)
    return lax.psum_scatter(
        partial_sum.astype(jnp.bfloat16), "head", scatter_dimension=1, tiled=True)


def solution(mesh):
    placed = (
        P("ctx", "head"),
        P("ctx", "head"),
        P("ctx", "head"),
        P("ctx", "head"),
        P("ctx", "head"),
        P(),
        P("ctx", "head", None),
    )
    return jax.shard_map(
        functools.partial(shards, mesh.shape["ctx"]),
        mesh=mesh, in_specs=placed, out_specs=P("ctx", "head"), check_vma=False)
```

time: 466 us -> 246 us (0.53)
  waiting for transfers between devices: 300 us -> 58.2 us
  Pallas kernels: 0 us -> 148 us
  matrix products: 72.1 us -> 13.2 us
  other arithmetic: 32.3 us -> 1.19 us
  starting transfers between devices: 29.7 us -> 0.04 us
  local copies, waits for them, and re-layouts: 18.1 us -> 11.5 us
    ppermute x6 -> x0, waiting for transfers between devices: 255 us -> none  [from_behind(): return lax.ppermute(array, axis, pairs)]
    pallas_call x0 -> x3, Pallas kernels: none -> 148 us  [the longest x1 114 us: reduce_window(): pl.pallas_call(functools.partial(reduce_kernel, n), out_shape=jax.ShapeDt...]
    dot_general x6 -> x1, matrix products: 72.1 us -> 13.2 us  [shards(): lax.dot_general(combined, weights, (((1,), (1,)), ((), ())), preferred_el...]
    ppermute x6 -> x0, starting transfers between devices: 29.6 us -> none  [from_behind(): return lax.ppermute(array, axis, pairs)]
    reduce_sum x4 -> x0, other arithmetic: 16.9 us -> none  [the longest x1 14.4 us: shards(): jnp.sum(jnp.where(allowed[None, None], jnp.exp(scores - row_max), 0.0), a...]
    reduce_scatter x1, waiting for transfers between devices: 44.5 us -> 58.1 us  [shards(): lax.psum_scatter(partial_sum.astype(jnp.bfloat16), 'head', scatter_dimens...]
    reshape x3 -> x1, local copies, waits for them, and re-layouts: 5.59 us -> 0.8 us  [shards(): dq.reshape(tile, heads_here, GROUP * HD)]
    unnamed x37 -> x18, local copies, waits for them, and re-layouts: 8.94 us -> 9.92 us
  transfers between devices with their start and end apart: 8 -> 2, of which waited for: 7 -> 1; matrix products, arithmetic and copies ran while one was open for 22% -> 1% of each run, Pallas kernels for 0% -> 60%
where the time goes in v1:
time: 246 us
  Pallas kernels  148 us (60%)
  waiting for transfers between devices  58.2 us (24%)
  between operations  14.1 us (6%)
  matrix products  13.2 us (5%)
  local copies, waits for them, and re-layouts  11.5 us (5%)
    pallas_call x1, Pallas kernels, reduce_window(): pl.pallas_call(functools.partial(reduce_kernel, n), out_shape=jax.ShapeDt...  114 us
    reduce_scatter x1, waiting for transfers between devices, shards(): lax.psum_scatter(partial_sum.astype(jnp.bfloat16), 'head', scatter_dimens...  58.1 us
    pallas_call x1, Pallas kernels, gather_window(): pl.pallas_call(functools.partial(gather_kernel, n), out_shape=jax.ShapeDt...  22.2 us
    dot_general x1, matrix products, shards(): lax.dot_general(combined, weights, (((1,), (1,)), ((), ())), preferred_el...  13.2 us
    pallas_call x1, Pallas kernels, attention(): pl.pallas_call(attention_kernel, grid_spec=pltpu.PrefetchScalarGridSpec(n...  11.8 us
    unnamed x18, local copies, waits for them, and re-layouts  9.92 us
  transfers between devices with their start and end apart: 2, of which 1 were waited for; matrix products, arithmetic and copies ran while one was open for 1% of the time, Pallas kernels for 60%

profile of v1, /device:TPU:0, one launch (start us, length us, event | category | flops | bytes accessed | tf_op | source)
XLA Modules:
  0.0 246.2 jit_solution(8086094694297197685)
XLA Ops:
  6.5 0.0 all-gather.2.cloned.1.call-start
  6.5 0.0 copy-start.7
  6.5 0.0 copy-start.5
  6.5 0.0 copy-start.6
  6.5 2.9 %copy.12 = bf16[32,8,4,768]{3,1,2,0:T(8,128)(2,1)} copy(bf16[32,8,4,768]{3,2,1,0:T(4,128)(2,1)} %bitcast.18) | data formatting | bytes 3145728
  9.4 0.0 all-gather.2.cloned.1.call-update
  9.5 0.0 reduce-scatter.2.cloned.1.call-start
  9.5 0.0 copy-done.7
  9.5 0.1 copy.10
  9.7 0.1 reduce
  9.8 0.1 select_reduce_fusion
  9.9 0.5 slice.9
  10.9 0.0 copy-done.5
  10.9 0.0 copy-done.6
  11.0 0.1 pad_maximum_fusion.1.kv_ref
  11.0 0.0 copy-start.2
  11.0 0.0 copy-start.3
  11.0 22.2 %shard_map.73.kv_ref = bf16[12,2,256,512]{3,2,1,0:T(8,128)(2,1)S(1)} custom-call(bf16[2,256,512]{2,1,0:T(8,128)(2,1)S(1)} %pad_maximum_fusion.1.kv_ref), custom_call_target="tpu_custom_call" | custom-call | tf_op jit(solution)/shard_map/pallas_call | solution.py:139
  33.3 0.0 copy-start
  33.3 2.7 %copy-done = bf16[12,2,256,512]{3,2,1,0:T(8,128)(2,1)} copy-done((bf16[12,2,256,512]{3,2,1,0:T(8,128)(2,1)}, bf16[12,2,256,512]{3,2,1,0:T(8,128)(2,1)S(1)}, u32[]{:S(2)}) %copy-start) | copy-done | bytes 6291480
  36.0 0.1 pad_add_fusion.info
  36.1 0.0 copy-done.2
  36.1 0.0 copy-done.3
  36.1 0.0 copy-start.4
  36.1 1.2 copy-done.4
  37.3 11.8 %shard_map.74 = (bf16[256,2048]{1,0:T(8,128)(2,1)S(1)}, bf16[12,2,256,512]{3,2,1,0:T(8,128)(2,1)}) custom-call(s32[3]{0:T(128)S(1)} %pad_add_fusion.info, bf16[256,2048]{1,0:T(8,128)(2,1)S(1)} %copy-done.2, bf16[256,2048]{1,0:T(8,128)(2,1)S(1)} %copy-done.3, bf16[256,2048]{1,0:T(8,128)(2,1)S(1)} %copy-done.4, bf16[12,2,256,512]{3,2,1,0:T(8,128)(2,1)} %copy-done, ...), custom_call_target="tpu_custom_call" | custom-call | flops 16106127360 | bytes 16777216 | tf_op jit(solution)/shard_map/pallas_call | solution.py:313
  49.1 0.0 copy-start.1
  49.1 2.8 %copy-done.1 = bf16[12,2,256,512]{3,2,1,0:T(8,128)(2,1)S(1)} copy-done((bf16[12,2,256,512]{3,2,1,0:T(8,128)(2,1)S(1)}, bf16[12,2,256,512]{3,2,1,0:T(8,128)(2,1)}, u32[]{:S(2)}) %copy-start.1) | copy-done | bytes 6291480
  51.9 114.0 %shard_map.75 = bf16[2,256,512]{2,1,0:T(8,128)(2,1)S(1)} custom-call(bf16[12,2,256,512]{3,2,1,0:T(8,128)(2,1)S(1)} %copy-done.1), custom_call_target="tpu_custom_call" | custom-call | tf_op jit(solution)/shard_map/pallas_call | solution.py:237
  166.0 0.1 reshape_squeeze.6
  166.0 0.1 reshape_squeeze.7
  166.1 0.8 reshape.50
  166.9 0.8 pad_maximum_fusion
  167.7 0.3 copy.11
  168.0 0.0 all-gather.2.cloned.1.call-done
  168.1 13.2 %convolution_convert_fusion = bf16[256,4096]{1,0:T(8,128)(2,1)} fusion(bf16[256,3072]{1,0:T(8,128)(2,1)S(1)} %bitcast.19, bf16[4096,3072]{1,0:T(8,128)(2,1)} %all-gather.2.cloned.1.call-done), kind=kOutput, calls=%fused_computation | convolution fusion | flops 6443499520 | bytes 28835840 | tf_op jit(solution)/shard_map/dot_general | solution.py:361
  181.3 0.0 reduce-scatter.2.cloned.1.call-update
  181.3 58.1 %reduce-scatter.2.cloned.1.call-done = bf16[256,2048]{1,0:T(8,128)(2,1)} async-done(((bf16[256,4096]{1,0:T(8,128)(2,1)}), bf16[256,2048]{1,0:T(8,128)(2,1)}) %reduce-scatter.2.cloned.1.call-update) | async-done | bytes 1048592 | tf_op jit(solution)/shard_map/reduce_scatter | solution.py:363
  (6 shorter events, 0.1 us)
Async XLA Ops:
  6.5 161.5 %all-gather.2.cloned.1.call-start = ((), (), s32[]{:S(2)}) async-start(), calls=%async_computation.1 | async-start | bytes 26738688 | tf_op jit(solution)/shard_map/all_gather | solution.py:342
  6.5 3.0 %copy-start.7 = (s32[16]{0:T(128)S(1)}, s32[16]{0:T(128)}, u32[]{:S(2)}) copy-start(s32[16]{0:T(128)} %param.12) | copy-start | bytes 196
  6.5 4.4 %copy-start.5 = (bf16[256,512]{1,0:T(8,128)(2,1)S(1)}, bf16[256,512]{1,0:T(8,128)(2,1)}, u32[]{:S(2)}) copy-start(bf16[256,512]{1,0:T(8,128)(2,1)} %param.9) | copy-start | bytes 786436
  6.5 4.4 %copy-start.6 = (bf16[256,512]{1,0:T(8,128)(2,1)S(1)}, bf16[256,512]{1,0:T(8,128)(2,1)}, u32[]{:S(2)}) copy-start(bf16[256,512]{1,0:T(8,128)(2,1)} %param.8) | copy-start | bytes 786436
  9.5 229.9 %reduce-scatter.2.cloned.1.call-start = ((), (), s32[]{:S(2)}) async-start(), calls=%async_computation.2 | async-start | bytes 3145728 | tf_op jit(solution)/shard_map/reduce_scatter | solution.py:363
  11.0 25.1 %copy-start.2 = (bf16[256,2048]{1,0:T(8,128)(2,1)S(1)}, bf16[256,2048]{1,0:T(8,128)(2,1)}, u32[]{:S(2)}) copy-start(bf16[256,2048]{1,0:T(8,128)(2,1)} %q_ref.1) | copy-start | bytes 3145732
  11.0 25.1 %copy-start.3 = (bf16[256,2048]{1,0:T(8,128)(2,1)S(1)}, bf16[256,2048]{1,0:T(8,128)(2,1)}, u32[]{:S(2)}) copy-start(bf16[256,2048]{1,0:T(8,128)(2,1)} %do_ref.1) | copy-start | bytes 3145732
  33.3 2.7 %copy-start = (bf16[12,2,256,512]{3,2,1,0:T(8,128)(2,1)}, bf16[12,2,256,512]{3,2,1,0:T(8,128)(2,1)S(1)}, u32[]{:S(2)}) copy-start(bf16[12,2,256,512]{3,2,1,0:T(8,128)(2,1)S(1)} %shard_map.73.kv_ref) | copy-start | bytes 18874372
  36.1 1.2 copy-start.4
  49.1 2.8 %copy-start.1 = (bf16[12,2,256,512]{3,2,1,0:T(8,128)(2,1)S(1)}, bf16[12,2,256,512]{3,2,1,0:T(8,128)(2,1)}, u32[]{:S(2)}) copy-start(bf16[12,2,256,512]{3,2,1,0:T(8,128)(2,1)} %get-tuple-element.8.g_ref) | copy-start | bytes 18874372
Sparse Core Ops, SparseCore 0:
  9.6 142.2 all-gather.1
  181.4 57.9 reduce-scatter.1

commit v2 on v1

--- a/solution.py
+++ b/solution.py
@@ -335,12 +335,126 @@
     )(info, q, do, ao, window, rows)
 
 
-def shards(n, queries, keys, values, out_grad, attn_out, lengths, proj_weight):
+def project_kernel(heads, dq_ref, g_ref, w_ref, out_ref, rows, came, keep, sent, got, total,
+                   c_send, c_recv, y_send, y_recv, o_send, o_recv):
+    c = lax.axis_index("ctx")
+    y = lax.axis_index("head")
+    b, k = (c // 2) % 2, c % 2
+    other, sib = c + 2 - 4 * b, c + 1 - 2 * k
+    owners = (c, sib, other, other + 1 - 2 * k)
+    mine = 2 * b + k
+    width = w_ref.shape[0] // heads
+    wide = GROUP * HD
+    barrier = pltpu.get_barrier_semaphore()
+    for peer in owners[1:]:
+        pl.semaphore_signal(barrier, inc=1, device_id={"ctx": peer}, device_id_type=MESH)
+    for d in range(1, heads):
+        pl.semaphore_signal(barrier, inc=1, device_id={"head": lax.rem(y + d, heads)},
+                            device_id_type=MESH)
+    pl.semaphore_wait(barrier, 3 + heads - 1)
+
+    for g in range(dq_ref.shape[1] // wide):
+        at = g * (wide + 2 * HD)
+        rows[:, at:at + wide] = dq_ref[:, g * wide:(g + 1) * wide]
+        rows[:, at + wide:at + wide + HD] = g_ref[0, :, g * HD:(g + 1) * HD]
+        rows[:, at + wide + HD:at + wide + 2 * HD] = g_ref[1, :, g * HD:(g + 1) * HD]
+
+    to_other = remote(rows, came.at[1], c_send.at[1], c_recv.at[1], other)
+    to_sib = remote(rows, came.at[0], c_send.at[0], c_recv.at[0], sib)
+    onward = remote(came.at[1], came.at[2], c_send.at[2], c_recv.at[2], sib)
+    to_other.start()
+    to_sib.start()
+
+    def swap(r, d):
+        return pltpu.make_async_remote_copy(
+            src_ref=sent.at[r, d - 1], dst_ref=got.at[r, d - 1],
+            send_sem=y_send.at[r, d - 1], recv_sem=y_recv.at[r, d - 1],
+            device_id={"head": lax.rem(y + d, heads)}, device_id_type=MESH)
+
+    def home(r):
+        return remote(total.at[r - 1], out_ref.at[mine], o_send.at[r - 1], o_recv.at[r - 1],
+                      owners[r])
+
+    def weight(p):
+        return w_ref[pl.ds(pl.multiple_of(p * width, width), width), :]
+
+    def finish(r):
+        value = keep[r]
+        for d in range(1, heads):
+            swap(r, d).wait_recv()
+            value = value + got[r, d - 1].astype(jnp.float32)
+        if r == 0:
+            out_ref[mine] = value.astype(out_ref.dtype)
+        else:
+            total[r - 1] = value.astype(total.dtype)
+            home(r).start()
+
+    for r in range(QUAD):
+        if r == 1:
+            to_sib.wait_recv()
+        elif r == 2:
+            to_other.wait_recv()
+            onward.start()
+        elif r == 3:
+            onward.wait_recv()
+        token_rows = rows if r == 0 else came.at[r - 1]
+        for d in range(1, heads):
+            sent[r, d - 1] = dot(
+                token_rows[...], weight(lax.rem(y + d, heads)), 1, 1).astype(sent.dtype)
+            swap(r, d).start()
+        keep[r] = dot(token_rows[...], weight(y), 1, 1)
+        if r > 0:
+            finish(r - 1)
+    finish(QUAD - 1)
+
+    to_sib.wait_send()
+    to_other.wait_send()
+    onward.wait_send()
+    for r in range(QUAD):
+        for d in range(1, heads):
+            swap(r, d).wait_send()
+        if r > 0:
+            home(r).wait_send()
+            home(r).wait_recv()
+
+
+def project(heads, dq, grads, weights):
+    tile = dq.shape[0]
+    depth = weights.shape[1]
+    width = weights.shape[0] // heads
+    low, peers = dq.dtype, max(heads - 1, 1)
+    vmem = pl.BlockSpec(memory_space=pltpu.VMEM)
+    return pl.pallas_call(
+        functools.partial(project_kernel, heads),
+        out_shape=jax.ShapeDtypeStruct((QUAD, tile, width), low),
+        in_specs=[vmem] * 3,
+        out_specs=vmem,
+        scratch_shapes=[
+            pltpu.VMEM((tile, depth), low),
+            pltpu.VMEM((3, tile, depth), low),
+            pltpu.VMEM((QUAD, tile, width), jnp.float32),
+            pltpu.VMEM((QUAD, peers, tile, width), low),
+            pltpu.VMEM((QUAD, peers, tile, width), low),
+            pltpu.VMEM((3, tile, width), low),
+            pltpu.SemaphoreType.DMA((3,)),
+            pltpu.SemaphoreType.DMA((3,)),
+            pltpu.SemaphoreType.DMA((QUAD, peers)),
+            pltpu.SemaphoreType.DMA((QUAD, peers)),
+            pltpu.SemaphoreType.DMA((3,)),
+            pltpu.SemaphoreType.DMA((3,)),
+        ],
+        compiler_params=pltpu.CompilerParams(
+            collective_id=2, has_side_effects=True, vmem_limit_bytes=48 * 1024 * 1024),
+    )(dq, grads, weights)
+
+
+def shards(n, heads, queries, keys, values, out_grad, attn_out, lengths, proj_weight):
     tile = queries.shape[0]
-    heads_here = keys.shape[1] // HD
     position = lax.axis_index("ctx")
+    lines = [list(range(r, n, QUAD)) for r in range(QUAD)]
     weights = lax.all_gather(
-        proj_weight.reshape(proj_weight.shape[0], -1), "ctx", axis=0, tiled=True)
+        proj_weight.reshape(proj_weight.shape[0], -1), "ctx", axis=0, tiled=True,
+        axis_index_groups=lines)
     window = gather_window(n, jnp.stack([keys, values]))
 
     ends = jnp.cumsum(lengths)
@@ -354,14 +468,11 @@
     rows = jnp.tile(rows, (1, GROUP))
     dq, parts = attention(info, queries, out_grad, attn_out, window, rows)
     grads = reduce_window(n, parts)
-    combined = jnp.concatenate(
-        [dq.reshape(tile, heads_here, GROUP * HD),
-         grads[0].reshape(tile, heads_here, HD),
-         grads[1].reshape(tile, heads_here, HD)], axis=2).reshape(tile, -1)
-    partial_sum = lax.dot_general(
-        combined, weights, (((1,), (1,)), ((), ())), preferred_element_type=jnp.float32)
-    return lax.psum_scatter(
-        partial_sum.astype(jnp.bfloat16), "head", scatter_dimension=1, tiled=True)
+    done = project(heads, dq, grads, weights)
+    members, _, width = done.shape
+    blocks = weights.shape[0] // proj_weight.shape[0] // heads
+    done = done.reshape(members, tile, blocks, width // blocks)
+    return jnp.transpose(done, (1, 2, 0, 3)).reshape(tile, members * width)
 
 
 def solution(mesh):
@@ -375,5 +486,5 @@
         P("ctx", "head", None),
     )
     return jax.shard_map(
-        functools.partial(shards, mesh.shape["ctx"]),
+        functools.partial(shards, mesh.shape["ctx"], mesh.shape["head"]),
         mesh=mesh, in_specs=placed, out_specs=P("ctx", "head"), check_vma=False)

time: 246 us -> 240 us (0.976)
  the two profiles are of different devices: /device:TPU:0 before, /device:TPU:9 now
where the time goes in v2:
time: 240 us
  Pallas kernels  209 us (87%)
  local copies, waits for them, and re-layouts  15.4 us (6%)
  between operations  14.1 us (6%)
    pallas_call x1, Pallas kernels, project(): pl.pallas_call(functools.partial(project_kernel, heads), out_shape=jax.Sh...  71.4 us
    pallas_call x1, Pallas kernels, gather_window(): pl.pallas_call(functools.partial(gather_kernel, n), out_shape=jax.ShapeDt...  63.5 us
    pallas_call x1, Pallas kernels, reduce_window(): pl.pallas_call(functools.partial(reduce_kernel, n), out_shape=jax.ShapeDt...  57.2 us
    pallas_call x1, Pallas kernels, attention(): pl.pallas_call(attention_kernel, grid_spec=pltpu.PrefetchScalarGridSpec(n...  16.7 us
    unnamed x11, local copies, waits for them, and re-layouts  10.9 us
  transfers between devices with their start and end apart: 1, of which 0 were waited for; matrix products, arithmetic and copies ran while one was open for 1% of the time, Pallas kernels for 57%

profile of v2, /device:TPU:9, one launch (start us, length us, event | category | flops | bytes accessed | tf_op | source)
XLA Modules:
  0.0 239.8 jit_solution(9453296117135678040)
XLA Ops:
  6.5 0.0 all-gather.2.cloned.1.call-start
  6.5 0.0 copy-start.2
  6.5 2.9 %copy.14 = bf16[32,8,4,768]{3,1,2,0:T(8,128)(2,1)} copy(bf16[32,8,4,768]{3,2,1,0:T(4,128)(2,1)} %bitcast.15) | data formatting | bytes 3145728
  9.5 0.0 all-gather.2.cloned.1.call-update
  9.5 0.7 copy.12
  10.3 0.1 reduce
  10.4 0.1 select_reduce_fusion
  10.5 0.5 slice.3
  11.7 1.1 pad_maximum_fusion.kv_ref
  12.8 63.5 %shard_map.73.kv_ref = bf16[12,2,256,512]{3,2,1,0:T(8,128)(2,1)S(1)} custom-call(bf16[2,256,512]{2,1,0:T(8,128)(2,1)S(1)} %pad_maximum_fusion.kv_ref), custom_call_target="tpu_custom_call" | custom-call | tf_op jit(solution)/shard_map/pallas_call | solution.py:139
  76.3 0.0 copy-start
  76.3 2.7 %copy-done = bf16[12,2,256,512]{3,2,1,0:T(8,128)(2,1)} copy-done((bf16[12,2,256,512]{3,2,1,0:T(8,128)(2,1)}, bf16[12,2,256,512]{3,2,1,0:T(8,128)(2,1)S(1)}, u32[]{:S(2)}) %copy-start) | copy-done | bytes 6291480
  79.0 0.1 pad_add_fusion.info
  79.1 0.0 copy-done.2
  79.1 0.0 copy-start.3
  79.1 1.2 copy-done.3
  80.3 0.0 copy-start.4
  80.4 1.2 copy-done.4
  81.6 16.7 %shard_map.74 = (bf16[256,2048]{1,0:T(8,128)(2,1)S(1)}, bf16[12,2,256,512]{3,2,1,0:T(8,128)(2,1)}) custom-call(s32[3]{0:T(128)S(1)} %pad_add_fusion.info, bf16[256,2048]{1,0:T(8,128)(2,1)S(1)} %copy-done.2, bf16[256,2048]{1,0:T(8,128)(2,1)S(1)} %copy-done.3, bf16[256,2048]{1,0:T(8,128)(2,1)S(1)} %copy-done.4, bf16[12,2,256,512]{3,2,1,0:T(8,128)(2,1)} %copy-done, ...), custom_call_target="tpu_custom_call" | custom-call | flops 16106127360 | bytes 16777216 | tf_op jit(solution)/shard_map/pallas_call | solution.py:313
  98.3 0.0 copy-start.1
  98.3 2.8 %copy-done.1 = bf16[12,2,256,512]{3,2,1,0:T(8,128)(2,1)S(1)} copy-done((bf16[12,2,256,512]{3,2,1,0:T(8,128)(2,1)S(1)}, bf16[12,2,256,512]{3,2,1,0:T(8,128)(2,1)}, u32[]{:S(2)}) %copy-start.1) | copy-done | bytes 6291480
  101.1 57.2 %shard_map.75.g_ref = bf16[2,256,512]{2,1,0:T(8,128)(2,1)S(1)} custom-call(bf16[12,2,256,512]{3,2,1,0:T(8,128)(2,1)S(1)} %copy-done.1), custom_call_target="tpu_custom_call" | custom-call | tf_op jit(solution)/shard_map/pallas_call | solution.py:237
  158.3 0.0 all-gather.2.cloned.1.call-done.w_ref
  158.3 71.4 %shard_map.76 = bf16[4,256,512]{2,1,0:T(8,128)(2,1)S(1)} custom-call(bf16[256,2048]{1,0:T(8,128)(2,1)S(1)} %get-tuple-element.7.dq_ref, bf16[2,256,512]{2,1,0:T(8,128)(2,1)S(1)} %shard_map.75.g_ref, bf16[1024,3072]{1,0:T(8,128)(2,1)} %all-gather.2.cloned.1.call-done.w_ref), custom_call_target="tpu_custom_call" | custom-call | tf_op jit(solution)/shard_map/pallas_call | solution.py:427
  229.7 0.3 reshape.51
  230.0 1.4 copy.13
  231.4 1.6 reshape.52
  (5 shorter events, 0.1 us)
Async XLA Ops:
  6.5 151.8 %all-gather.2.cloned.1.call-start = ((), (), s32[]{:S(2)}) async-start(), calls=%async_computation | async-start | bytes 7864320 | tf_op jit(solution)/shard_map/all_gather | solution.py:455
  6.5 72.6 %copy-start.2 = (bf16[256,2048]{1,0:T(8,128)(2,1)S(1)}, bf16[256,2048]{1,0:T(8,128)(2,1)}, u32[]{:S(2)}) copy-start(bf16[256,2048]{1,0:T(8,128)(2,1)} %q_ref.1) | copy-start | bytes 3145732
  76.3 2.7 %copy-start = (bf16[12,2,256,512]{3,2,1,0:T(8,128)(2,1)}, bf16[12,2,256,512]{3,2,1,0:T(8,128)(2,1)S(1)}, u32[]{:S(2)}) copy-start(bf16[12,2,256,512]{3,2,1,0:T(8,128)(2,1)S(1)} %shard_map.73.kv_ref) | copy-start | bytes 18874372
  79.1 1.2 copy-start.3
  80.3 1.2 copy-start.4
  98.3 2.8 %copy-start.1 = (bf16[12,2,256,512]{3,2,1,0:T(8,128)(2,1)S(1)}, bf16[12,2,256,512]{3,2,1,0:T(8,128)(2,1)}, u32[]{:S(2)}) copy-start(bf16[12,2,256,512]{3,2,1,0:T(8,128)(2,1)} %get-tuple-element.8.g_ref) | copy-start | bytes 18874372
Sparse Core Ops, SparseCore 0:
  9.6 128.8 all-gather.1

commit v3 on v2

--- a/solution.py
+++ b/solution.py
@@ -151,7 +151,8 @@
     )(kv)
 
 
-def reduce_kernel(n, g_ref, out_ref, from_f, from_s, from_x, from_z, sum_x, sum_z, send, recv):
+def reduce_kernel(n, g_ref, dq_ref, out_ref, came, from_f, from_s, from_x, from_z, sum_x, sum_z,
+                  send, recv, q_send, q_recv):
     c, m, b, k, quads = place(n)
     down, other, sib = c - QUAD, c + 2 - 4 * b, c + 1 - 2 * k
     greet(n)
@@ -179,6 +180,10 @@
 
     def z_copy(dz):
         return remote(sum_z.at[dz], from_z.at[dz - 1], send.at[dz, 0], recv.at[dz - 1, 0], down)
+
+    to_sib = remote(dq_ref, came.at[0], q_send.at[0], q_recv.at[0], sib)
+    to_other = remote(dq_ref, came.at[1], q_send.at[1], q_recv.at[1], other)
+    onward = remote(came.at[1], came.at[2], q_send.at[2], q_recv.at[2], sib)
 
     for dz in (2, 1, 0):
         @pl.when(has(dz))
@@ -196,6 +201,8 @@
                          + from_f[dz].astype(jnp.float32)).astype(sum_x.dtype)
             x_copy(dz).start()
 
+    to_other.start()
+    to_sib.start()
     for dz in (2, 1, 0):
         @pl.when(has(dz))
         def _(dz=dz):
@@ -218,6 +225,11 @@
                 z_copy(dz).start()
 
     out_ref[...] = sum_z[0]
+    to_other.wait_recv()
+    onward.start()
+    to_sib.wait()
+    to_other.wait_send()
+    onward.wait()
     for dz in range(3):
         @pl.when(has(dz))
         def _(dz=dz):
@@ -231,21 +243,24 @@
                 z_copy(dz).wait_send()
 
 
-def reduce_window(n, parts):
+def reduce_window(n, parts, dq):
     one = parts.shape[1:]
     vmem = pl.BlockSpec(memory_space=pltpu.VMEM)
     return pl.pallas_call(
         functools.partial(reduce_kernel, n),
-        out_shape=jax.ShapeDtypeStruct(one, parts.dtype),
-        in_specs=[vmem],
-        out_specs=vmem,
+        out_shape=[jax.ShapeDtypeStruct(one, parts.dtype),
+                   jax.ShapeDtypeStruct((3,) + dq.shape, dq.dtype)],
+        in_specs=[vmem, vmem],
+        out_specs=[vmem, vmem],
         scratch_shapes=[pltpu.VMEM((count,) + one, parts.dtype) for count in (3, 3, 3, 2, 3, 3)] + [
             pltpu.SemaphoreType.DMA((3, 4)),
             pltpu.SemaphoreType.DMA((3, 4)),
+            pltpu.SemaphoreType.DMA((3,)),
+            pltpu.SemaphoreType.DMA((3,)),
         ],
         compiler_params=pltpu.CompilerParams(
             collective_id=1, has_side_effects=True, vmem_limit_bytes=40 * 1024 * 1024),
-    )(parts)
+    )(parts, dq)
 
 
 def dot(a, b, ca, cb, **kw):
@@ -335,7 +350,7 @@
     )(info, q, do, ao, window, rows)
 
 
-def project_kernel(heads, dq_ref, g_ref, w_ref, out_ref, rows, came, keep, sent, got, total,
+def project_kernel(heads, dq_ref, quad_ref, g_ref, w_ref, out_ref, rows, came, keep, sent, got, total,
                    c_send, c_recv, y_send, y_recv, o_send, o_recv):
     c = lax.axis_index("ctx")
     y = lax.axis_index("head")
@@ -353,14 +368,16 @@
                             device_id_type=MESH)
     pl.semaphore_wait(barrier, 3 + heads - 1)
 
-    for g in range(dq_ref.shape[1] // wide):
-        at = g * (wide + 2 * HD)
-        rows[:, at:at + wide] = dq_ref[:, g * wide:(g + 1) * wide]
-        rows[:, at + wide:at + wide + HD] = g_ref[0, :, g * HD:(g + 1) * HD]
-        rows[:, at + wide + HD:at + wide + 2 * HD] = g_ref[1, :, g * HD:(g + 1) * HD]
-
-    to_other = remote(rows, came.at[1], c_send.at[1], c_recv.at[1], other)
-    to_sib = remote(rows, came.at[0], c_send.at[0], c_recv.at[0], sib)
+    def assemble(r):
+        heads_of, pair = (dq_ref, g_ref) if r == 0 else (quad_ref.at[r - 1], came.at[r - 1])
+        for g in range(dq_ref.shape[1] // wide):
+            at = g * (wide + 2 * HD)
+            rows[r, :, at:at + wide] = heads_of[:, g * wide:(g + 1) * wide]
+            rows[r, :, at + wide:at + wide + HD] = pair[0, :, g * HD:(g + 1) * HD]
+            rows[r, :, at + wide + HD:at + wide + 2 * HD] = pair[1, :, g * HD:(g + 1) * HD]
+
+    to_other = remote(g_ref, came.at[1], c_send.at[1], c_recv.at[1], other)
+    to_sib = remote(g_ref, came.at[0], c_send.at[0], c_recv.at[0], sib)
     onward = remote(came.at[1], came.at[2], c_send.at[2], c_recv.at[2], sib)
     to_other.start()
     to_sib.start()
@@ -397,12 +414,12 @@
             onward.start()
         elif r == 3:
             onward.wait_recv()
-        token_rows = rows if r == 0 else came.at[r - 1]
+        assemble(r)
         for d in range(1, heads):
             sent[r, d - 1] = dot(
-                token_rows[...], weight(lax.rem(y + d, heads)), 1, 1).astype(sent.dtype)
+                rows[r], weight(lax.rem(y + d, heads)), 1, 1).astype(sent.dtype)
             swap(r, d).start()
-        keep[r] = dot(token_rows[...], weight(y), 1, 1)
+        keep[r] = dot(rows[r], weight(y), 1, 1)
         if r > 0:
             finish(r - 1)
     finish(QUAD - 1)
@@ -418,7 +435,7 @@
             home(r).wait_recv()
 
 
-def project(heads, dq, grads, weights):
+def project(heads, dq, dq_quad, grads, weights):
     tile = dq.shape[0]
     depth = weights.shape[1]
     width = weights.shape[0] // heads
@@ -427,11 +444,11 @@
     return pl.pallas_call(
         functools.partial(project_kernel, heads),
         out_shape=jax.ShapeDtypeStruct((QUAD, tile, width), low),
-        in_specs=[vmem] * 3,
+        in_specs=[vmem] * 4,
         out_specs=vmem,
         scratch_shapes=[
-            pltpu.VMEM((tile, depth), low),
-            pltpu.VMEM((3, tile, depth), low),
+            pltpu.VMEM((QUAD, tile, depth), low),
+            pltpu.VMEM((3,) + grads.shape, low),
             pltpu.VMEM((QUAD, tile, width), jnp.float32),
             pltpu.VMEM((QUAD, peers, tile, width), low),
             pltpu.VMEM((QUAD, peers, tile, width), low),
@@ -445,17 +462,17 @@
         ],
         compiler_params=pltpu.CompilerParams(
             collective_id=2, has_side_effects=True, vmem_limit_bytes=48 * 1024 * 1024),
-    )(dq, grads, weights)
+    )(dq, dq_quad, grads, weights)
 
 
 def shards(n, heads, queries, keys, values, out_grad, attn_out, lengths, proj_weight):
     tile = queries.shape[0]
     position = lax.axis_index("ctx")
+    window = gather_window(n, jnp.stack([keys, values]))
     lines = [list(range(r, n, QUAD)) for r in range(QUAD)]
-    weights = lax.all_gather(
-        proj_weight.reshape(proj_weight.shape[0], -1), "ctx", axis=0, tiled=True,
-        axis_index_groups=lines)
-    window = gather_window(n, jnp.stack([keys, values]))
+    window, held = lax.optimization_barrier(
+        (window, proj_weight.reshape(proj_weight.shape[0], -1)))
+    weights = lax.all_gather(held, "ctx", axis=0, tiled=True, axis_index_groups=lines)
 
     ends = jnp.cumsum(lengths)
     query_pos = position * tile + jnp.arange(tile, dtype=jnp.int32)
@@ -467,8 +484,8 @@
     rows = jnp.stack([start, query_pos] + [query_pos] * 6).astype(jnp.int32)
     rows = jnp.tile(rows, (1, GROUP))
     dq, parts = attention(info, queries, out_grad, attn_out, window, rows)
-    grads = reduce_window(n, parts)
-    done = project(heads, dq, grads, weights)
+    grads, dq_quad = reduce_window(n, parts, dq)
+    done = project(heads, dq, dq_quad, grads, weights)
     members, _, width = done.shape
     blocks = weights.shape[0] // proj_weight.shape[0] // heads
     done = done.reshape(members, tile, blocks, width // blocks)

time: 240 us -> 241 us (level)
  the two profiles are of different devices: /device:TPU:9 before, /device:TPU:0 now
where the time goes in v3:
time: 241 us; the launch traced here: 239 us
  Pallas kernels  187 us (78%)
  waiting for transfers between devices  21 us (9%)
  local copies, waits for them, and re-layouts  15.5 us (6%)
  between operations  14.1 us (6%)
    pallas_call x1, Pallas kernels, reduce_window(): pl.pallas_call(functools.partial(reduce_kernel, n), out_shape=[jax.ShapeD...  124 us
    pallas_call x1, Pallas kernels, project(): pl.pallas_call(functools.partial(project_kernel, heads), out_shape=jax.Sh...  36.8 us
    all_gather x1, waiting for transfers between devices, shards(): lax.all_gather(held, 'ctx', axis=0, tiled=True, axis_index_groups=lines)  20.9 us
    pallas_call x1, Pallas kernels, gather_window(): pl.pallas_call(functools.partial(gather_kernel, n), out_shape=jax.ShapeDt...  14.5 us
    pallas_call x1, Pallas kernels, attention(): pl.pallas_call(attention_kernel, grid_spec=pltpu.PrefetchScalarGridSpec(n...  11.8 us
    unnamed x19, local copies, waits for them, and re-layouts  11.7 us
  transfers between devices with their start and end apart: 1, of which 1 were waited for; matrix products, arithmetic and copies ran while one was open for 0% of the time, Pallas kernels for 57%

profile of v3, /device:TPU:0, one launch (start us, length us, event | category | flops | bytes accessed | tf_op | source)
XLA Modules:
  0.0 239.5 jit_solution(14813482136698760961)
XLA Ops:
  6.5 0.0 all-gather.2.cloned.1.call-start
  6.5 0.0 copy-start.7
  6.5 0.0 copy-start.8
  6.5 0.0 copy-start.4
  6.5 0.0 copy-start.5
  6.5 1.2 pad_maximum_fusion.kv_ref
  7.8 14.5 %shard_map.73.kv_ref = bf16[12,2,256,512]{3,2,1,0:T(8,128)(2,1)S(1)} custom-call(bf16[2,256,512]{2,1,0:T(8,128)(2,1)S(1)} %pad_maximum_fusion.kv_ref), custom_call_target="tpu_custom_call" | custom-call | tf_op jit(solution)/shard_map/pallas_call | solution.py:139
  22.3 0.0 copy-start.1
  22.3 2.6 %copy-done.1 = bf16[12,2,256,512]{3,2,1,0:T(8,128)(2,1)} copy-done((bf16[12,2,256,512]{3,2,1,0:T(8,128)(2,1)}, bf16[12,2,256,512]{3,2,1,0:T(8,128)(2,1)S(1)}, u32[]{:S(2)}) %copy-start.1) | copy-done | bytes 6291480
  25.0 0.0 copy-done.7
  25.0 1.5 copy.14
  26.4 0.0 all-gather.2.cloned.1.call-update
  26.5 0.0 copy-done.8
  26.5 0.1 copy.12
  26.6 0.1 reduce
  26.7 0.1 select_reduce_fusion
  26.8 0.5 slice.3
  27.9 0.1 pad_add_fusion.info
  28.0 0.0 copy-done.4
  28.0 0.0 copy-done.5
  28.0 0.0 copy-start.6
  28.0 1.2 copy-done.6
  29.3 11.8 %shard_map.74 = (bf16[256,2048]{1,0:T(8,128)(2,1)S(1)}, bf16[12,2,256,512]{3,2,1,0:T(8,128)(2,1)}) custom-call(s32[3]{0:T(128)S(1)} %pad_add_fusion.info, bf16[256,2048]{1,0:T(8,128)(2,1)S(1)} %copy-done.4, bf16[256,2048]{1,0:T(8,128)(2,1)S(1)} %copy-done.5, bf16[256,2048]{1,0:T(8,128)(2,1)S(1)} %copy-done.6, bf16[12,2,256,512]{3,2,1,0:T(8,128)(2,1)} %copy-done.1, ...), custom_call_target="tpu_custom_call" | custom-call | flops 16106127360 | bytes 16777216 | tf_op jit(solution)/shard_map/pallas_call | solution.py:328
  41.0 0.0 copy-start
  41.0 2.8 %copy-done = bf16[12,2,256,512]{3,2,1,0:T(8,128)(2,1)S(1)} copy-done((bf16[12,2,256,512]{3,2,1,0:T(8,128)(2,1)S(1)}, bf16[12,2,256,512]{3,2,1,0:T(8,128)(2,1)}, u32[]{:S(2)}) %copy-start) | copy-done | bytes 6291480
  43.8 124.2 %shard_map.75 = (bf16[2,256,512]{2,1,0:T(8,128)(2,1)S(1)}, bf16[3,256,2048]{2,1,0:T(8,128)(2,1)S(1)}) custom-call(bf16[12,2,256,512]{3,2,1,0:T(8,128)(2,1)S(1)} %copy-done, bf16[256,2048]{1,0:T(8,128)(2,1)S(1)} %get-tuple-element.12.dq_ref), custom_call_target="tpu_custom_call" | custom-call | tf_op jit(solution)/shard_map/pallas_call | solution.py:249
  168.1 0.0 copy-start.2
  168.1 1.7 copy-done.2
  169.8 20.9 %all-gather.2.cloned.1.call-done.w_ref = bf16[1024,3072]{1,0:T(8,128)(2,1)} async-done(((bf16[256,3072]{1,0:T(8,128)(2,1)}), bf16[1024,3072]{1,0:T(8,128)(2,1)}) %all-gather.2.cloned.1.call-update) | async-done | bytes 6291472 | tf_op jit(solution)/shard_map/all_gather | solution.py:475
  190.7 0.0 copy-start.3
  190.7 1.9 copy-done.3
  192.6 36.8 %shard_map.76 = bf16[4,256,512]{2,1,0:T(8,128)(2,1)S(1)} custom-call(bf16[256,2048]{1,0:T(8,128)(2,1)S(1)} %get-tuple-element.12.dq_ref, bf16[3,256,2048]{2,1,0:T(8,128)(2,1)S(1)} %copy-done.3, bf16[2,256,512]{2,1,0:T(8,128)(2,1)S(1)} %get-tuple-element.15.g_ref, bf16[1024,3072]{1,0:T(8,128)(2,1)} %all-gather.2.cloned.1.call-done.w_ref), custom_call_target="tpu_custom_call" | custom-call | tf_op jit(solution)/shard_map/pallas_call | solution.py:444
  229.4 0.3 reshape.51
  229.7 1.4 copy.13
  231.1 1.6 reshape.52
  (5 shorter events, 0.1 us)
Async XLA Ops:
  6.5 184.2 %all-gather.2.cloned.1.call-start = ((), (), s32[]{:S(2)}) async-start(), calls=%async_computation | async-start | bytes 7864320 | tf_op jit(solution)/shard_map/all_gather | solution.py:475
  6.5 18.4 %copy-start.7 = (bf16[256,4,768]{2,1,0:T(4,128)(2,1)S(1)}, bf16[256,4,768]{2,1,0:T(4,128)(2,1)}, u32[]{:S(2)}) copy-start(bf16[256,4,768]{2,1,0:T(4,128)(2,1)} %param.13) | copy-start | bytes 4718596
  6.5 19.9 %copy-start.8 = (s32[16]{0:T(128)S(1)}, s32[16]{0:T(128)}, u32[]{:S(2)}) copy-start(s32[16]{0:T(128)} %param.12) | copy-start | bytes 196
  6.5 21.5 %copy-start.4 = (bf16[256,2048]{1,0:T(8,128)(2,1)S(1)}, bf16[256,2048]{1,0:T(8,128)(2,1)}, u32[]{:S(2)}) copy-start(bf16[256,2048]{1,0:T(8,128)(2,1)} %q_ref.1) | copy-start | bytes 3145732
  6.5 21.5 %copy-start.5 = (bf16[256,2048]{1,0:T(8,128)(2,1)S(1)}, bf16[256,2048]{1,0:T(8,128)(2,1)}, u32[]{:S(2)}) copy-start(bf16[256,2048]{1,0:T(8,128)(2,1)} %do_ref.1) | copy-start | bytes 3145732
  22.3 2.6 %copy-start.1 = (bf16[12,2,256,512]{3,2,1,0:T(8,128)(2,1)}, bf16[12,2,256,512]{3,2,1,0:T(8,128)(2,1)S(1)}, u32[]{:S(2)}) copy-start(bf16[12,2,256,512]{3,2,1,0:T(8,128)(2,1)S(1)} %shard_map.73.kv_ref) | copy-start | bytes 18874372
  28.0 1.2 copy-start.6
  41.0 2.8 %copy-start = (bf16[12,2,256,512]{3,2,1,0:T(8,128)(2,1)S(1)}, bf16[12,2,256,512]{3,2,1,0:T(8,128)(2,1)}, u32[]{:S(2)}) copy-start(bf16[12,2,256,512]{3,2,1,0:T(8,128)(2,1)} %get-tuple-element.13.g_ref) | copy-start | bytes 18874372
  168.1 1.7 copy-start.2
  190.7 1.9 copy-start.3
Sparse Core Ops, SparseCore 0:
  26.6 164.0 all-gather.1
